TPU v7x, 32 devices: a whole 2x2x4 slice. The times are simulated.
32 devices in a mesh: pole: 4 (over y, x), row: 2 (over core), col: 4 (over z).
Axes of the slice: x: 2, y: 2, z: 4, core: 2. Of those that a mesh axis runs over, the one named last changes fastest.
Arguments:
- hamiltonian_panel: bfloat16 [6144, 512], P(('row', 'col'), 'pole'), may hold values from -0.005859375 to 0.005859375
- margin_panel: bfloat16 [6144, 512], P(('row', 'col'), 'pole'), may hold values from -0.0029296875 to 0.0029296875
- shifts: float32 [4, 2], P('pole'), may hold values from -2 to 2
- weights: float32 [4, 2], P('pole'), may hold values from 0.5 to 2
- pivot_inverse: float32 [4, 2, 512, 512], P('pole'), may hold values from -6 to 6
- selected_inverse: bfloat16 [4, 2, 6144, 6144], P('pole', None, 'row', 'col'), may hold values from -6 to 6
Outputs:
- inverse_column: float32 [4, 6144, 2, 512], P('pole', ('row', 'col'))
- inverse_pivot: float32 [4, 2, 512, 512], P('pole')
- density_column: float32 [6144, 512], P(('row', 'col'), 'pole')
- density_pivot: float32 [512, 512], P('pole')
All inputs are finite; a program needn't handle non-finite values.
Results may differ from a plain program's by a relative error of at most 0.0037.
Values may be sent and summed in bfloat16 or wider, within the bound.
A program may use at most 128 MiB of HBM per device.

v0:
```python
import jax
import jax.numpy as jnp
from jax import lax
from jax.sharding import PartitionSpec as P

PANEL = 512


def precise(left, right):
    return jnp.dot(left, right, precision=lax.Precision.HIGHEST, preferred_element_type=jnp.float32)


def factor_panel(hamiltonian, margin, shift, inverse):
    hamiltonian_f = hamiltonian.astype(jnp.float32)
    margin_f = margin.astype(jnp.float32)
    real_part = hamiltonian_f - shift[0] * margin_f
    imag_part = -shift[1] * margin_f
    lower_real = precise(real_part, inverse[0]) - precise(imag_part, inverse[1])
    lower_imag = precise(real_part, inverse[1]) + precise(imag_part, inverse[0])
    return jnp.stack([lower_real, lower_imag], axis=1).astype(jnp.bfloat16)


def apply_block(block_real, block_imag, lower):
    width = lower.shape[2]
    flat = lower.reshape(lower.shape[0], 2 * width)
    first = jnp.dot(block_real, flat, preferred_element_type=jnp.float32)
    second = jnp.dot(block_imag, flat, preferred_element_type=jnp.float32)
    return -jnp.stack(
        [first[:, :width] - second[:, width:], first[:, width:] + second[:, :width]], axis=1
    )


def pivot_term(lower, column):
    width = lower.shape[2]
    left = lower.astype(jnp.float32).reshape(lower.shape[0], 2 * width)
    right = column.reshape(column.shape[0], 2 * width)
    square = lax.dot_general(
        left,
        right,
        (((0,), (0,)), ((), ())),
        precision=lax.Precision.HIGHEST,
        preferred_element_type=jnp.float32,
    )
    return jnp.stack(
        [
            square[:width, :width] - square[width:, width:],
            square[:width, width:] + square[width:, :width],
        ]
    )


def body(hamiltonian_panel, margin_panel, shifts, weights, pivot_inverse, selected_inverse):
    shift = shifts[0]
    weight = weights[0]
    inverse = pivot_inverse[0]
    block = selected_inverse[0]
    span = block.shape[2]
    column_index = lax.axis_index("col")
    both = (
        lax.all_gather(hamiltonian_panel, "pole", axis=1, tiled=True),
        lax.all_gather(margin_panel, "pole", axis=1, tiled=True),
    )
    owned = factor_panel(both[0], both[1], shift, inverse)
    gathered = lax.all_gather(owned, ("row", "col"), axis=0, tiled=True)
    needed = lax.dynamic_slice_in_dim(gathered, column_index * span, span, 0)
    block_real = block[0]
    block_imag = block[1]
    column = lax.psum_scatter(
        apply_block(block_real, block_imag, needed), "col", scatter_dimension=0, tiled=True
    )
    pivot = inverse - lax.psum(pivot_term(owned, column), ("row", "col"))
    column_density = weight[0] * column[:, 0] - weight[1] * column[:, 1]
    pivot_density = weight[0] * pivot[0] - weight[1] * pivot[1]
    totals = lax.psum((column_density, pivot_density), "pole")
    portion = PANEL // lax.axis_size("pole")
    slot = lax.axis_index("pole")
    column_share = lax.dynamic_slice_in_dim(totals[0], slot * portion, portion, 1)
    pivot_share = lax.dynamic_slice_in_dim(totals[1], slot * portion, portion, 0)
    return (column[None], pivot[None], column_share, pivot_share)


def solution(mesh):
    return jax.shard_map(
        body,
        mesh=mesh,
        in_specs=(
            P(("row", "col"), "pole"),
            P(("row", "col"), "pole"),
            P("pole", None),
            P("pole", None),
            P("pole", None, None, None),
            P("pole", None, "row", "col"),
        ),
        out_specs=(
            P("pole", ("row", "col"), None, None),
            P("pole", None, None, None),
            P(("row", "col"), "pole"),
            P("pole", None),
        ),
        check_vma=False,
    )
```

profile of v0, /device:TPU:0, one launch (start us, length us, event | category | flops | bytes accessed | tf_op | source)
XLA Modules:
  0.0 594.3 jit_solution(16487910491604722457)
XLA Ops:
  7.2 13.8 %all_gather.10 = bf16[768,512]{1,0:T(8,128)(2,1)S(1)} all-gather(bf16[768,128]{1,0:T(8,128)(2,1)} %param.7), channel_id=1, replica_groups=mesh['pole'=4,'row'=2,'col'=4] {'pole'}, dimensions={1}, use_global_device_ids=true | all-gather | bytes 983040 | tf_op jit(solution)/shard_map/all_gather | solution.py:61
  21.0 1.3 fusion.42
  22.3 11.1 %all_gather.9 = bf16[768,512]{1,0:T(8,128)(2,1)S(1)} all-gather(bf16[768,128]{1,0:T(8,128)(2,1)} %param.6), channel_id=1, replica_groups=mesh['pole'=4,'row'=2,'col'=4] {'pole'}, dimensions={1}, use_global_device_ids=true | all-gather | bytes 983040 | tf_op jit(solution)/shard_map/all_gather | solution.py:60
  33.4 5.0 fusion.21
  38.4 3.7 fusion.19
  42.8 3.1 fusion.23
  45.8 3.1 fusion.24
  48.9 1.5 pad_maximum_fusion.1
  50.4 117.1 %all-gather.2.cloned.1.call-done = bf16[6144,2,512]{0,2,1:T(8,128)(2,1)} async-done(((bf16[768,2,512]{0,2,1:T(8,128)(2,1)}), bf16[6144,2,512]{0,2,1:T(8,128)(2,1)}) %all-gather.2.cloned.1.call-update) | async-done | bytes 12582928 | tf_op jit(solution)/shard_map/all_gather | solution.py:64
  167.5 2.1 constant_dynamic-slice_fusion.2
  169.6 12.5 %fusion.6 = f32[3072,1024]{0,1:T(8,128)S(1)} fusion(bf16[1536,1024]{0,1:T(8,128)(2,1)S(1)} %bitcast.59, bf16[1,2,3072,1536]{3,2,1,0:T(8,128)(2,1)} %param.11), kind=kOutput, calls=%fused_computation.7 | convolution fusion | flops 9663676416 | bytes 25165824 | tf_op jit(solution)/shard_map/dot_general | solution.py:26
  182.1 15.2 %fusion.9 = f32[3072,1024]{0,1:T(8,128)} fusion(bf16[1536,1024]{0,1:T(8,128)(2,1)S(1)} %bitcast.60, bf16[1,2,3072,1536]{3,2,1,0:T(8,128)(2,1)} %param.11), kind=kOutput, calls=%fused_computation.8 | convolution fusion | flops 9663676416 | bytes 25165824 | tf_op jit(solution)/shard_map/dot_general | solution.py:27
  197.3 7.4 %fusion.13 = (f32[3072,1,512]{0,2,1:T(8,128)S(1)}, f32[3072,1,512]{0,2,1:T(8,128)}) fusion(f32[3072,1024]{0,1:T(8,128)} %fusion.9, f32[3072,1024]{0,1:T(8,128)S(1)} %fusion.6), kind=kLoop, calls=%fused_computation.12 | loop fusion | flops 3145728 | bytes 37748736 | tf_op jit(solution)/shard_map/stack | solution.py:28
  204.8 9.2 %maximum_negate_fusion = f32[3072,2,512]{0,2,1:T(8,128)} fusion(f32[3072,1,512]{0,2,1:T(8,128)} %get-tuple-element.11, f32[3072,1,512]{0,2,1:T(8,128)S(1)} %get-tuple-element.10), kind=kLoop, calls=%fused_computation | loop fusion | flops 6291456 | bytes 25165824 | tf_op jit(solution)/shard_map/neg | solution.py:28
  214.0 0.3 all-reduce.4.cloned.1.call-start
  214.2 209.9 %reduce-scatter.2.cloned.1.call-done = f32[768,2,512]{0,2,1:T(8,128)} async-done(((f32[3072,2,512]{0,2,1:T(8,128)}), f32[768,2,512]{0,2,1:T(8,128)}) %reduce-scatter.2.cloned.1.call-update) | async-done | bytes 3145744 | tf_op jit(solution)/shard_map/reduce_scatter | solution.py:68
  424.2 7.1 %fusion.43 = f32[1024,1024]{1,0:T(8,128)S(1)} fusion(bf16[768,1024]{0,1:T(8,128)(2,1)S(1)} %bitcast.58, f32[768,1024]{0,1:T(8,128)} %bitcast.55), kind=kOutput, calls=%fused_computation.56 | convolution fusion | flops 9663676416 | bytes 8912896 | tf_op jit(solution)/shard_map/dot_general | solution.py:37
  431.3 0.5 fusion.28
  431.8 1.5 pad_maximum_fusion
  433.4 0.0 all-reduce.6.cloned.1.call-start
  433.4 0.6 copy-done.5
  434.0 0.6 fusion.41
  434.6 4.7 fusion.18
  439.3 60.3 %all-reduce.4.cloned.1.call-done = f32[2,512,512]{2,1,0:T(8,128)} async-done(((f32[2,512,512]{2,1,0:T(8,128)}), f32[2,512,512]{2,1,0:T(8,128)}) %all-reduce.4.cloned.1.call-update) | async-done | bytes 2097168 | tf_op jit(solution)/shard_map/psum | solution.py:71
  499.5 2.1 bitcast_subtract_fusion
  501.6 1.3 copy-done.3
  502.9 2.8 fusion.26
  505.8 3.4 copy.10
  509.1 75.0 %all-reduce.6.cloned.1.call-done = (f32[768,512]{0,1:T(8,128)}, f32[512,512]{1,0:T(8,128)}) async-done(((f32[768,512]{0,1:T(8,128)}, f32[512,512]{1,0:T(8,128)}), (f32[768,512]{0,1:T(8,128)}, f32[512,512]{1,0:T(8,128)})) %all-reduce.6.cloned.1.call-update) | async-done | bytes 2621456 | tf_op jit(solution)/shard_map/psum | solution.py:74
  584.2 1.0 constant_dynamic-slice_fusion.1
  585.2 0.9 copy.11
  586.1 1.7 constant_dynamic-slice_fusion
  (16 shorter events, 0.2 us)
Async XLA Ops:
  7.2 160.4 %all-gather.2.cloned.1.call-start = ((), (), s32[]{:S(2)}) async-start(), calls=%async_computation.1 | async-start | bytes 14155776 | tf_op jit(solution)/shard_map/all_gather | solution.py:64
  33.4 5.0 copy-start
  50.4 373.8 %reduce-scatter.2.cloned.1.call-start = ((), (), s32[]{:S(2)}) async-start(), calls=%async_computation.2 | async-start | bytes 15728640 | tf_op jit(solution)/shard_map/reduce_scatter | solution.py:68
  213.9 210.2 %copy-start.4 = (bf16[768,2,512]{0,2,1:T(8,128)(2,1)S(1)}, bf16[768,2,512]{0,2,1:T(8,128)(2,1)}, u32[]{:S(2)}) copy-start(bf16[768,2,512]{0,2,1:T(8,128)(2,1)} %pad_maximum_fusion.1) | copy-start | bytes 4718596
  214.0 285.5 %all-reduce.4.cloned.1.call-start = ((), (), s32[]{:S(2)}) async-start(), calls=%async_computation.3 | async-start | bytes 4194304 | tf_op jit(solution)/shard_map/psum | solution.py:71
  433.3 0.7 copy-start.5
  433.4 150.8 %all-reduce.6.cloned.1.call-start = ((), (), s32[]{:S(2)}) async-start(), calls=%async_computation.4 | async-start | bytes 5242880 | tf_op jit(solution)/shard_map/psum | solution.py:74
  434.6 64.9 %copy-start.1 = (f32[1,2,512,512]{3,2,1,0:T(8,128)S(1)}, f32[1,2,512,512]{3,2,1,0:T(8,128)}, u32[]{:S(2)}) copy-start(f32[1,2,512,512]{3,2,1,0:T(8,128)} %param.10) | copy-start | bytes 6291460
  501.6 1.3 copy-start.3
  502.9 2.9 copy-start.2
Sparse Core Ops, SparseCore 0:
  50.5 116.9 all-gather.1
  214.1 210.0 reduce-scatter.1
  433.5 65.9 all-reduce.3
  505.9 78.2 all-reduce.5
where the time goes:
time: 595 us; the launch traced here: 594 us
  waiting for transfers between devices  462 us (78%)
  matrix products  49.6 us (8%)
  other arithmetic  29.7 us (5%)
  blocking collectives  24.9 us (4%)
  between operations  14.5 us (2%)
  local copies, waits for them, and re-layouts  12.9 us (2%)
    reduce_scatter x1, waiting for transfers between devices, body(): lax.psum_scatter(apply_block(block_real, block_imag, needed), 'col', scat...  210 us
    all_gather x1, waiting for transfers between devices, body(): gathered = lax.all_gather(owned, ('row', 'col'), axis=0, tiled=True)  117 us
    psum x1, waiting for transfers between devices, body(): totals = lax.psum((column_density, pivot_density), 'pole')  75 us
    psum x1, waiting for transfers between devices, body(): pivot = inverse - lax.psum(pivot_term(owned, column), ('row', 'col'))  60.3 us
    dot_general x1, matrix products, apply_block(): second = jnp.dot(block_imag, flat, preferred_element_type=jnp.float32)  15.2 us
    dot_general x4, matrix products, precise(): jnp.dot(left, right, precision=lax.Precision.HIGHEST, preferred_element_t...  14.8 us
    all_gather x1, blocking collectives, body(): lax.all_gather(margin_panel, 'pole', axis=1, tiled=True)  13.8 us
    dot_general x1, matrix products, apply_block(): first = jnp.dot(block_real, flat, preferred_element_type=jnp.float32)  12.5 us
  transfers between devices with their start and end apart: 4, of which 4 were waited for; matrix products, arithmetic and copies ran while one was open for 1% of the time, Pallas kernels for 0%

commit v1 on v0

--- a/solution.py
+++ b/solution.py
@@ -68,7 +68,8 @@
     column = lax.psum_scatter(
         apply_block(block_real, block_imag, needed), "col", scatter_dimension=0, tiled=True
     )
-    pivot = inverse - lax.psum(pivot_term(owned, column), ("row", "col"))
+    _reach_tokens = lambda x0: jax.lax.psum(jax.lax.psum(x0, axis_name="col"), "row")
+    pivot = inverse - _reach_tokens(pivot_term(owned, column))
     column_density = weight[0] * column[:, 0] - weight[1] * column[:, 1]
     pivot_density = weight[0] * pivot[0] - weight[1] * pivot[1]
     totals = lax.psum((column_density, pivot_density), "pole")

time: 595 us -> 640 us (1.076)
  waiting for transfers between devices: 462 us -> 508 us
    psum x1 -> x2, waiting for transfers between devices: 60.3 us -> 105 us  [the longest x1 87.6 us: body(): jax.lax.psum(x0, axis_name='col')]
  transfers between devices with their start and end apart: 4 -> 5, of which waited for: 4 -> 5; matrix products, arithmetic and copies ran while one was open for 1% -> 1% of each run, Pallas kernels for 0% -> 0%
where the time goes in v1:
time: 640 us
  waiting for transfers between devices  508 us (79%)
  matrix products  49.6 us (8%)
  other arithmetic  29.6 us (5%)
  blocking collectives  24.9 us (4%)
  between operations  14.5 us (2%)
  local copies, waits for them, and re-layouts  12.3 us (2%)
    reduce_scatter x1, waiting for transfers between devices, body(): lax.psum_scatter(apply_block(block_real, block_imag, needed), 'col', scat...  210 us
    all_gather x1, waiting for transfers between devices, body(): gathered = lax.all_gather(owned, ('row', 'col'), axis=0, tiled=True)  117 us
    psum x1, waiting for transfers between devices, body(): jax.lax.psum(x0, axis_name='col')  87.6 us
    psum x1, waiting for transfers between devices, body(): totals = lax.psum((column_density, pivot_density), 'pole')  76.6 us
    psum x1, waiting for transfers between devices, body(): jax.lax.psum(jax.lax.psum(x0, axis_name='col'), 'row')  17.1 us
    dot_general x1, matrix products, apply_block(): second = jnp.dot(block_imag, flat, preferred_element_type=jnp.float32)  15.2 us
    dot_general x4, matrix products, precise(): jnp.dot(left, right, precision=lax.Precision.HIGHEST, preferred_element_t...  14.8 us
    all_gather x1, blocking collectives, body(): lax.all_gather(margin_panel, 'pole', axis=1, tiled=True)  13.8 us
  transfers between devices with their start and end apart: 5, of which 5 were waited for; matrix products, arithmetic and copies ran while one was open for 1% of the time, Pallas kernels for 0%

profile of v1, /device:TPU:0, one launch (start us, length us, event | category | flops | bytes accessed | tf_op | source)
XLA Modules:
  0.0 639.9 jit_solution(4639005313834560345)
XLA Ops:
  7.2 13.8 %all_gather.10 = bf16[768,512]{1,0:T(8,128)(2,1)S(1)} all-gather(bf16[768,128]{1,0:T(8,128)(2,1)} %param.7), channel_id=1, replica_groups=mesh['pole'=4,'row'=2,'col'=4] {'pole'}, dimensions={1}, use_global_device_ids=true | all-gather | bytes 983040 | tf_op jit(solution)/shard_map/all_gather | solution.py:61
  21.0 1.3 fusion.42
  22.3 11.1 %all_gather.9 = bf16[768,512]{1,0:T(8,128)(2,1)S(1)} all-gather(bf16[768,128]{1,0:T(8,128)(2,1)} %param.6), channel_id=1, replica_groups=mesh['pole'=4,'row'=2,'col'=4] {'pole'}, dimensions={1}, use_global_device_ids=true | all-gather | bytes 983040 | tf_op jit(solution)/shard_map/all_gather | solution.py:60
  33.4 5.0 fusion.21
  38.4 3.7 fusion.19
  42.8 3.1 fusion.23
  45.8 3.1 fusion.24
  48.9 1.5 pad_maximum_fusion.1
  50.4 0.0 reduce-scatter.2.cloned.1.call-start
  50.4 117.1 %all-gather.2.cloned.1.call-done = bf16[6144,2,512]{0,2,1:T(8,128)(2,1)} async-done(((bf16[768,2,512]{0,2,1:T(8,128)(2,1)}), bf16[6144,2,512]{0,2,1:T(8,128)(2,1)}) %all-gather.2.cloned.1.call-update) | async-done | bytes 12582928 | tf_op jit(solution)/shard_map/all_gather | solution.py:64
  167.5 2.1 constant_dynamic-slice_fusion.2
  169.6 12.5 %fusion.6 = f32[3072,1024]{0,1:T(8,128)S(1)} fusion(bf16[1536,1024]{0,1:T(8,128)(2,1)S(1)} %bitcast.59, bf16[1,2,3072,1536]{3,2,1,0:T(8,128)(2,1)} %param.11), kind=kOutput, calls=%fused_computation.7 | convolution fusion | flops 9663676416 | bytes 25165824 | tf_op jit(solution)/shard_map/dot_general | solution.py:26
  182.1 15.2 %fusion.9 = f32[3072,1024]{0,1:T(8,128)} fusion(bf16[1536,1024]{0,1:T(8,128)(2,1)S(1)} %bitcast.60, bf16[1,2,3072,1536]{3,2,1,0:T(8,128)(2,1)} %param.11), kind=kOutput, calls=%fused_computation.8 | convolution fusion | flops 9663676416 | bytes 25165824 | tf_op jit(solution)/shard_map/dot_general | solution.py:27
  197.3 7.4 %fusion.13 = (f32[3072,1,512]{0,2,1:T(8,128)S(1)}, f32[3072,1,512]{0,2,1:T(8,128)}) fusion(f32[3072,1024]{0,1:T(8,128)} %fusion.9, f32[3072,1024]{0,1:T(8,128)S(1)} %fusion.6), kind=kLoop, calls=%fused_computation.12 | loop fusion | flops 3145728 | bytes 37748736 | tf_op jit(solution)/shard_map/stack | solution.py:28
  204.8 9.2 %maximum_negate_fusion = f32[3072,2,512]{0,2,1:T(8,128)} fusion(f32[3072,1,512]{0,2,1:T(8,128)} %get-tuple-element.11, f32[3072,1,512]{0,2,1:T(8,128)S(1)} %get-tuple-element.10), kind=kLoop, calls=%fused_computation | loop fusion | flops 6291456 | bytes 25165824 | tf_op jit(solution)/shard_map/neg | solution.py:28
  214.0 0.3 all-reduce.5.cloned.1.call-start
  214.2 209.9 %reduce-scatter.2.cloned.1.call-done = f32[768,2,512]{0,2,1:T(8,128)} async-done(((f32[3072,2,512]{0,2,1:T(8,128)}), f32[768,2,512]{0,2,1:T(8,128)}) %reduce-scatter.2.cloned.1.call-update) | async-done | bytes 3145744 | tf_op jit(solution)/shard_map/reduce_scatter | solution.py:68
  424.2 7.1 %fusion.43 = f32[1024,1024]{1,0:T(8,128)S(1)} fusion(bf16[768,1024]{0,1:T(8,128)(2,1)S(1)} %bitcast.58, f32[768,1024]{0,1:T(8,128)} %bitcast.55), kind=kOutput, calls=%fused_computation.56 | convolution fusion | flops 9663676416 | bytes 8912896 | tf_op jit(solution)/shard_map/dot_general | solution.py:37
  431.3 0.5 fusion.28
  431.8 1.5 pad_maximum_fusion
  433.4 87.6 %all-reduce.5.cloned.1.call-done = f32[2,512,512]{2,1,0:T(8,128)} async-done(((f32[2,512,512]{2,1,0:T(8,128)}), f32[2,512,512]{2,1,0:T(8,128)}) %all-reduce.5.cloned.1.call-update) | async-done | bytes 2097168 | tf_op jit(solution)/shard_map/psum | solution.py:71
  521.1 0.6 fusion.41
  521.7 4.7 fusion.18
  526.4 17.1 %all-reduce.7.cloned.1.call-done = f32[2,512,512]{2,1,0:T(8,128)} async-done(((f32[2,512,512]{2,1,0:T(8,128)}), f32[2,512,512]{2,1,0:T(8,128)}) %all-reduce.7.cloned.1.call-update) | async-done | bytes 2097168 | tf_op jit(solution)/shard_map/psum | solution.py:71
  543.6 2.1 bitcast_subtract_fusion
  545.7 1.3 copy-done.3
  547.0 2.8 fusion.26
  549.8 3.4 copy.10
  553.2 76.6 %all-reduce.9.cloned.1.call-done = (f32[768,512]{0,1:T(8,128)}, f32[512,512]{1,0:T(8,128)}) async-done(((f32[768,512]{0,1:T(8,128)}, f32[512,512]{1,0:T(8,128)}), (f32[768,512]{0,1:T(8,128)}, f32[512,512]{1,0:T(8,128)})) %all-reduce.9.cloned.1.call-update) | async-done | bytes 2621456 | tf_op jit(solution)/shard_map/psum | solution.py:75
  629.7 1.0 constant_dynamic-slice_fusion.1
  630.8 0.9 copy.11
  631.7 1.7 constant_dynamic-slice_fusion
  (19 shorter events, 0.2 us)
Async XLA Ops:
  7.2 160.4 %all-gather.2.cloned.1.call-start = ((), (), s32[]{:S(2)}) async-start(), calls=%async_computation.1 | async-start | bytes 14155776 | tf_op jit(solution)/shard_map/all_gather | solution.py:64
  33.4 5.0 copy-start
  50.4 373.8 %reduce-scatter.2.cloned.1.call-start = ((), (), s32[]{:S(2)}) async-start(), calls=%async_computation.2 | async-start | bytes 15728640 | tf_op jit(solution)/shard_map/reduce_scatter | solution.py:68
  213.9 210.2 %copy-start.4 = (bf16[768,2,512]{0,2,1:T(8,128)(2,1)S(1)}, bf16[768,2,512]{0,2,1:T(8,128)(2,1)}, u32[]{:S(2)}) copy-start(bf16[768,2,512]{0,2,1:T(8,128)(2,1)} %pad_maximum_fusion.1) | copy-start | bytes 4718596
  214.0 307.1 %all-reduce.5.cloned.1.call-start = ((), (), s32[]{:S(2)}) async-start(), calls=%async_computation.3 | async-start | bytes 4194304 | tf_op jit(solution)/shard_map/psum | solution.py:71
  433.3 87.8 %copy-start.5 = (f32[1,2]{1,0:T(1,128)S(1)}, f32[1,2]{1,0:T(1,128)}, u32[]{:S(2)}) copy-start(f32[1,2]{1,0:T(1,128)} %param.9) | copy-start | bytes 28
  433.4 110.2 %all-reduce.7.cloned.1.call-start = ((), (), s32[]{:S(2)}) async-start(), calls=%async_computation.4 | async-start | bytes 4194304 | tf_op jit(solution)/shard_map/psum | solution.py:71
  521.1 108.7 %all-reduce.9.cloned.1.call-start = ((), (), s32[]{:S(2)}) async-start(), calls=%async_computation.5 | async-start | bytes 5242880 | tf_op jit(solution)/shard_map/psum | solution.py:75
  521.7 21.9 %copy-start.1 = (f32[1,2,512,512]{3,2,1,0:T(8,128)S(1)}, f32[1,2,512,512]{3,2,1,0:T(8,128)}, u32[]{:S(2)}) copy-start(f32[1,2,512,512]{3,2,1,0:T(8,128)} %param.10) | copy-start | bytes 6291460
  545.7 1.3 copy-start.3
  547.0 2.8 copy-start.2
Sparse Core Ops, SparseCore 0:
  50.5 116.9 all-gather.1
  214.1 210.0 reduce-scatter.1
  433.5 87.5 all-reduce.4
  523.4 20.1 all-reduce.6
  549.9 79.7 all-reduce.8
